TPU v7x, 32 devices: a whole 2x2x4 slice. The times are simulated.
32 devices in a mesh: sect: 2 (over y), batch: 8 (over z, core), head: 2 (over x).
Axes of the slice: x: 2, y: 2, z: 4, core: 2. Of those that a mesh axis runs over, the one named last changes fastest.
Arguments:
- queries: bfloat16 [48, 16, 512], P('batch', 'head', 'sect'), may hold values from -51 to 51
- newest_key_value: bfloat16 [48, 4, 256], P('batch'), may hold values from -5 to 5
- page_cache: bfloat16 [48, 256, 64, 256], P('batch', ('sect', 'head')), may hold values from -4 to 4
- lengths: int32 [48], P('batch'), may hold values from 2048 to 4096, as said below
- page_ids: int32 [48, 4, 32], P('batch'), may hold values from 0 to 63, as said below
- out_weight: bfloat16 [8192, 4096], P(('sect', 'head'), 'batch'), may hold values from -0.0625 to 0.0625
- residual: bfloat16 [48, 4096], P(None, 'batch'), may hold values from -2 to 2
- norm_gain: float32 [4096], P('batch'), may hold values from 0.25 to 1.75
- expert_ids: int32 [48, 8], replicated, may hold values from 0 to 63, all different within a row; in each aligned block of 48 rows (0 to 47, 48 to 95, ...) at most 12 rows name the same one
- route_weight: float32 [48, 8], replicated, may hold values from 0.1 to 1
- gate_up_weight: bfloat16 [32, 4096, 2, 3072], P(('sect', 'batch'), None, None, 'head'), may hold values from -0.09375 to 0.09375
- down_weight: bfloat16 [32, 3072, 4096], P(('sect', 'batch'), 'head'), may hold values from -0.15625 to 0.15625
Outputs:
- layer_out: bfloat16 [48, 4096], P(None, 'batch')
Inputs may be any that keep to these rules, and one draw needn't show every extreme that they name: `lengths`: some sequence holds exactly 4096 cached tokens and some exactly 2048. `page_ids`: each row lists 32 different pages in ascending order, all below the number of pages that hold the sequence's cached tokens, and always the last of those pages. `expert_ids`: each row names 8 different experts; over all rows no expert is named by more than 12 rows, a bound that some block reaches.
All inputs are finite; a program needn't handle non-finite values.
Results may differ from a plain program's by a relative error of at most 0.025.
Values may be sent and summed in bfloat16 or wider, within the bound.
A program may use at most 192 MiB of HBM per device.

v0:
```python
import math

import jax
import jax.numpy as jnp
from jax import lax
from jax.sharding import PartitionSpec as P

D = 4096
EXPERTS = 64


NEG_FILL = -1e30
NORM_EPS = 1e-06


def as_sent(shard):
    return jax.tree.map(lambda a: a.astype(jnp.bfloat16) if a.dtype == jnp.float32 else a, shard)


def from_partner(shard, axis, distance):
    return lax.ppermute(shard, axis, [(i, i ^ 1 << distance) for i in range(lax.axis_size(axis))])


def merge_pair(first, second):
    first_max, first_sum, first_acc = first
    second_max, second_sum, second_acc = second
    joined = jnp.maximum(first_max, second_max)
    first_factor = jnp.exp(first_max - joined)
    second_factor = jnp.exp(second_max - joined)
    return (
        joined,
        first_sum * first_factor + second_sum * second_factor,
        first_acc * first_factor[..., None] + second_acc * second_factor[..., None],
    )


def head_slice(partial_value, begin_at, span_size):
    return tuple(
        (lax.dynamic_slice_in_dim(member, begin_at, span_size, 1) for member in partial_value)
    )


def on_device(
    queries,
    newest_key_value,
    page_cache,
    lengths,
    page_ids,
    out_weight,
    residual,
    norm_gain,
    expert_ids,
    route_weight,
    gate_up_weight,
    down_weight,
):
    seq_count = queries.shape[0]
    head_dim = newest_key_value.shape[2] // 2
    kv_heads = newest_key_value.shape[1]
    sect_size = lax.axis_size("sect")
    head_size = lax.axis_size("head")
    batch_size = lax.axis_size("batch")
    group_size = sect_size * head_size // kv_heads
    position = lax.axis_index("sect") * head_size + lax.axis_index("head")
    kv_index = position // group_size
    quarter = position % group_size
    local_pages = page_cache.shape[1]
    page_len = page_cache.shape[2]
    scaling = 1.0 / math.sqrt(head_dim)
    all_heads = lax.all_gather(queries, "head", axis=1, tiled=True)
    kv_local = kv_index % (kv_heads // sect_size)
    group_query = lax.dynamic_slice_in_dim(all_heads, kv_local * head_dim, head_dim, 2)
    heads_dev = all_heads.shape[1] // group_size
    block_cols = heads_dev * head_dim
    chosen = lax.dynamic_index_in_dim(page_ids, kv_index, 1, keepdims=False)
    leading_page = quarter * local_pages
    page_number = jnp.broadcast_to(
        leading_page + jnp.arange(local_pages, dtype=jnp.int32), (seq_count, local_pages)
    )
    page_used = jnp.any(chosen[:, :, None] == page_number[:, None, :], axis=1)
    token_place = (
        page_number[:, :, None] * page_len + jnp.arange(page_len, dtype=jnp.int32)[None, None, :]
    )
    key_count = page_cache.shape[1] * page_len
    usable_pages = (page_used[:, :, None] & (token_place < lengths[:, None, None])).reshape(
        seq_count, key_count
    )
    gathered_keys = page_cache[..., :head_dim].reshape(seq_count, key_count, head_dim)
    gathered_values = page_cache[..., head_dim:].reshape(seq_count, key_count, head_dim)
    scores = (
        jnp.einsum("shd,skd->shk", group_query, gathered_keys, preferred_element_type=jnp.float32)
        * scaling
    )
    scores = jnp.where(usable_pages[:, None, :], scores, NEG_FILL)
    newest_entry = lax.dynamic_index_in_dim(newest_key_value, kv_index, 1, keepdims=False)
    fresh_score = (
        jnp.einsum(
            "shd,sd->sh",
            group_query,
            newest_entry[:, :head_dim],
            preferred_element_type=jnp.float32,
        )
        * scaling
    )
    leading = quarter == 0
    fresh_score = jnp.where(leading, fresh_score, NEG_FILL)
    running_max = jnp.maximum(jnp.max(scores, axis=2), fresh_score)
    weights = jnp.where(usable_pages[:, None, :], jnp.exp(scores - running_max[..., None]), 0.0)
    fresh_weight = jnp.where(leading, jnp.exp(fresh_score - running_max), 0.0)
    running_sum = jnp.sum(weights, axis=2) + fresh_weight
    weighted = jnp.einsum(
        "shk,skd->shd",
        weights.astype(jnp.bfloat16),
        gathered_values,
        preferred_element_type=jnp.float32,
    )
    weighted = weighted + fresh_weight.astype(jnp.bfloat16).astype(jnp.float32)[
        ..., None
    ] * newest_entry[:, None, head_dim:].astype(jnp.float32)
    partial_value = (running_max, running_sum, weighted)
    bit_count = group_size.bit_length() - 1
    for bit_index in range(bit_count):
        partner = from_partner(
            (as_sent(partial_value[0]), as_sent(partial_value[1]), as_sent(partial_value[2])),
            "head",
            bit_index,
        )
        partial_value = merge_pair(partial_value, partner)
    partial_value = head_slice(partial_value, quarter * heads_dev, heads_dev)
    attention = (
        (partial_value[2] / partial_value[1][..., None])
        .reshape(seq_count, block_cols)
        .astype(jnp.bfloat16)
    )
    head_terms = jnp.dot(
        lax.all_gather(attention, "batch", axis=0, tiled=True),
        out_weight,
        preferred_element_type=jnp.float32,
    )
    projected = lax.psum(head_terms.astype(jnp.bfloat16), ("sect", "head")).astype(jnp.float32)
    hidden_state = residual.astype(jnp.float32) + projected
    squares = lax.psum(jnp.sum(hidden_state * hidden_state, axis=1), "batch")
    inverse = lax.rsqrt(squares / D + NORM_EPS)
    normed = (hidden_state * inverse[:, None] * norm_gain[None, :]).astype(jnp.bfloat16)
    token_count, top_count = expert_ids.shape
    capacity = 2 * token_count * top_count // EXPERTS
    pair_local = gate_up_weight.shape[0]
    flat_ids = expert_ids.reshape(-1)
    one_hot = (flat_ids[:, None] == jnp.arange(EXPERTS, dtype=jnp.int32)[None, :]).astype(jnp.int32)
    earlier = jnp.cumsum(one_hot, axis=0) - one_hot
    rank_in = jnp.sum(earlier * one_hot, axis=1)
    sub_half = lax.axis_index("head") // (head_size // 2)
    pair_first = lax.axis_index("sect") * (batch_size * pair_local)
    local_pair = flat_ids // 2 - pair_first
    in_sect = (local_pair >= 0) & (local_pair < batch_size * pair_local)
    full_slot = (
        (local_pair // pair_local * 2 + flat_ids % 2) * pair_local + local_pair % pair_local
    ) * capacity + rank_in
    full_slot = jnp.where(in_sect, full_slot, -1)
    slot_dev = pair_local * capacity
    slot_total = batch_size * 2 * slot_dev
    send_count = batch_size * slot_dev
    matches = (
        full_slot.reshape(token_count, top_count)[None, :, :]
        == jnp.arange(slot_total, dtype=jnp.int32)[:, None, None]
    )
    selector_full = (
        jnp.any(matches, axis=2).astype(jnp.bfloat16).reshape(batch_size, 2, slot_dev, token_count)
    )
    selector = lax.dynamic_index_in_dim(selector_full, sub_half, 1, keepdims=False).reshape(
        send_count, token_count
    )
    coefficient = route_weight / jnp.sum(route_weight, axis=1, keepdims=True)
    combine_full = jnp.sum(jnp.where(matches, coefficient[None, :, :], 0.0), axis=2).T
    cols_dev = normed.shape[1]
    outgoing = jnp.dot(selector, normed, preferred_element_type=jnp.float32).astype(jnp.bfloat16)
    outgoing = outgoing.reshape(batch_size, pair_local, capacity, cols_dev)
    arrived = lax.all_to_all(outgoing, "batch", split_axis=0, concat_axis=3, tiled=True)[0]
    mixture = jnp.einsum(
        "ecd,edgf->ecgf", arrived, gate_up_weight, preferred_element_type=jnp.float32
    )
    activated = (jax.nn.silu(mixture[:, :, 0]) * mixture[:, :, 1]).astype(jnp.bfloat16)
    expert_part = jnp.einsum(
        "ecf,efd->ecd", activated, down_weight, preferred_element_type=jnp.float32
    )
    leaving = expert_part.reshape(1, slot_dev, batch_size, cols_dev)
    came_back = (
        lax.all_to_all(
            leaving.astype(jnp.bfloat16), "batch", split_axis=2, concat_axis=0, tiled=True
        )
        .astype(leaving.dtype)
        .reshape(send_count, cols_dev)
    )
    weights_used = lax.dynamic_index_in_dim(
        combine_full.reshape(token_count, batch_size, 2, slot_dev), sub_half, 2, keepdims=False
    )
    weights_used = weights_used.reshape(token_count, send_count)
    combined = jnp.dot(
        weights_used, came_back, precision=lax.Precision.HIGHEST, preferred_element_type=jnp.float32
    )
    expert_mix = lax.psum(combined.astype(jnp.bfloat16), ("sect", "head")).astype(jnp.float32)
    return (hidden_state + expert_mix).astype(jnp.bfloat16)


def solution(mesh):
    placed = (
        P("batch", "head", "sect"),
        P("batch", None, None),
        P("batch", ("sect", "head"), None, None),
        P("batch"),
        P("batch", None, None),
        P(("sect", "head"), "batch"),
        P(None, "batch"),
        P("batch"),
        P(),
        P(),
        P(("sect", "batch"), None, None, "head"),
        P(("sect", "batch"), "head", None),
    )
    return jax.shard_map(
        on_device, mesh=mesh, in_specs=placed, out_specs=P(None, "batch"), check_vma=False
    )
```

profile of v0, /device:TPU:0, one launch (start us, length us, event | category | flops | bytes accessed | tf_op | source)
XLA Modules:
  0.0 150.9 jit_solution(7628843917287937767)
XLA Ops:
  0.0 0.9 copy.67
  1.1 0.7 constant_dynamic-slice_fusion.3
  2.1 0.1 and.66
  2.4 11.4 %fusion.49 = (bf16[6,64,64,128]{3,2,1,0:T(8,128)(2,1)}, bf16[6,64,64,128]{3,2,1,0:T(8,128)(2,1)}) fusion(bf16[6,64,64,256]{3,2,1,0:T(8,128)(2,1)} %param.14), kind=kLoop, calls=%fused_computation.95 | loop fusion | bytes 25165824 | tf_op jit(solution)/shard_map/slice | solution.py:88
  13.8 5.4 %all_gather.6 = bf16[6,16,256]{2,1,0:T(8,128)(2,1)S(1)} all-gather(bf16[6,8,256]{2,1,0:T(8,128)(2,1)S(1)} %copy-done.4), channel_id=1, replica_groups=mesh['sect'=2,'batch'=8,'head'=2] {'head'}, dimensions={1}, use_global_device_ids=true | all-gather | bytes 73728 | tf_op jit(solution)/shard_map/all_gather | solution.py:70
  19.3 0.1 fusion.37
  19.5 4.8 %fusion.50 = (f32[6,16]{1,0:T(8,128)S(1)}, f32[6,16,4096]{2,1,0:T(8,128)S(1)}) fusion(bf16[6,4096,128]{2,1,0:T(8,128)(2,1)} %bitcast.87, bf16[6,16,256]{2,1,0:T(8,128)(2,1)S(1)} %all_gather.6, s32[]{:T(128)S(6)} %select_n.82, pred[6,4096]{1,0:T(8,128)(4,1)S(1)} %compare_and_fusion), kind=kOutput, calls=%fused_computation.96 | convolution fusion | flops 101842848 | bytes 7922052 | tf_op jit(solution)/shard_map/shd,skd->shk/dot_general | solution.py:91
  24.2 0.5 fusion.3
  24.8 1.1 fusion.6
  25.9 15.0 %all-gather = bf16[8,6,2048]{2,1,0:T(8,128)(2,1)S(1)} all-gather(bf16[1,6,2048]{2,1,0:T(8,128)(2,1)S(1)} %reshape.180), channel_id=1, replica_groups=mesh['sect'=2,'batch'=8,'head'=2] {'batch'}, dimensions={0}, use_global_device_ids=true | all-gather | bytes 221184 | tf_op jit(solution)/shard_map/all_gather | solution.py:136
  41.0 0.5 convolution_convert_fusion.3
  41.5 16.7 %psum.21 = bf16[48,512]{1,0:T(8,128)(2,1)S(1)} all-reduce(bf16[48,512]{1,0:T(8,128)(2,1)S(1)} %convolution_convert_fusion.3), channel_id=1, replica_groups=mesh['sect'=2,'batch'=8,'head'=2] {'sect','head'}, use_global_device_ids=true, to_apply=%region_3.4 | all-reduce | flops 24576 | bytes 98304 | tf_op jit(solution)/shard_map/psum | solution.py:140
  58.3 13.6 %psum.22 = f32[48]{0:T(128)S(1)} all-reduce(f32[48]{0:T(128)S(1)} %multiply_reduce_fusion), channel_id=1, replica_groups=mesh['sect'=2,'batch'=8,'head'=2] {'batch'}, use_global_device_ids=true, to_apply=%region_11.12 | all-reduce | flops 48 | bytes 384 | tf_op jit(solution)/shard_map/psum | solution.py:142
  72.0 0.9 reduce-window.6
  72.9 0.2 slice_reduce_fusion
  73.4 0.2 fusion.11
  73.7 0.2 copy.76
  73.9 0.3 convolution_convert_fusion.1
  74.2 0.9 copy.77
  75.1 3.6 %all-to-all-start = ((bf16[8,2,12,512]{3,1,2,0:T(2,128)(2,1)}), bf16[8,2,12,512]{3,1,2,0:T(2,128)(2,1)S(1)}, u32[]{:S(2)}, u32[]{:S(2)}) async-start(bf16[8,2,12,512]{3,1,2,0:T(2,128)(2,1)} %copy.77), calls=%async_computation | async-start | bytes 393216 | tf_op jit(solution)/shard_map/all_to_all | solution.py:178
  78.7 8.0 %all-to-all-done = bf16[8,2,12,512]{3,1,2,0:T(2,128)(2,1)S(1)} async-done(((bf16[8,2,12,512]{3,1,2,0:T(2,128)(2,1)}), bf16[8,2,12,512]{3,1,2,0:T(2,128)(2,1)S(1)}, u32[]{:S(2)}, u32[]{:S(2)}) %all-to-all-start) | async-done | bytes 196640 | tf_op jit(solution)/shard_map/all_to_all | solution.py:178
  86.8 0.1 reshape.185
  86.9 25.9 %fusion = f32[2,12,2,1536]{3,1,2,0:T(8,128)S(1)} fusion(bf16[2,4096,2,1536]{3,2,1,0:T(2,128)(2,1)} %param.22, bf16[2,12,4096,1]{2,1,0,3:T(8,128)(2,1)S(1)} %reshape.185), kind=kOutput, calls=%fused_computation | convolution fusion | flops 603979776 | bytes 50823168 | tf_op jit(solution)/shard_map/ecd,edgf->ecgf/dot_general | solution.py:179
  112.8 10.1 %convolution_convert_fusion = bf16[2,12,4096]{2,1,0:T(8,128)(2,1)S(1)} fusion(bf16[2,1536,4096]{2,1,0:T(8,128)(2,1)} %param.23, f32[2,12,2,1536]{3,1,2,0:T(8,128)S(1)} %fusion), kind=kOutput, calls=%fused_computation.4 | convolution fusion | flops 302309376 | bytes 25657344 | tf_op jit(solution)/shard_map/ecf,efd->ecd/dot_general | solution.py:183
  122.9 0.1 convert_element_type.84
  123.1 0.7 copy.82
  123.8 3.4 %all-to-all-start.1 = ((bf16[1,24,8,512]{3,1,0,2:T(8,128)(2,1)}), bf16[1,24,8,512]{3,1,0,2:T(8,128)(2,1)S(1)}, u32[]{:S(2)}, u32[]{:S(2)}) async-start(bf16[1,24,8,512]{3,1,0,2:T(8,128)(2,1)} %copy.82), calls=%async_computation.1 | async-start | bytes 393216 | tf_op jit(solution)/shard_map/all_to_all | solution.py:188
  127.3 0.2 select_reduce_fusion
  127.7 7.8 %all-to-all-done.1 = bf16[1,24,8,512]{3,1,0,2:T(8,128)(2,1)S(1)} async-done(((bf16[1,24,8,512]{3,1,0,2:T(8,128)(2,1)}), bf16[1,24,8,512]{3,1,0,2:T(8,128)(2,1)S(1)}, u32[]{:S(2)}, u32[]{:S(2)}) %all-to-all-start.1) | async-done | bytes 196640 | tf_op jit(solution)/shard_map/all_to_all | solution.py:188
  135.5 0.3 convolution_convert_fusion.2
  135.7 14.6 %psum.23 = bf16[48,512]{1,0:T(8,128)(2,1)S(1)} all-reduce(bf16[48,512]{1,0:T(8,128)(2,1)S(1)} %convolution_convert_fusion.2), channel_id=1, replica_groups=mesh['sect'=2,'batch'=8,'head'=2] {'sect','head'}, use_global_device_ids=true, to_apply=%region_12.13 | all-reduce | flops 24576 | bytes 98304 | tf_op jit(solution)/shard_map/psum | solution.py:201
  150.3 0.6 add_convert_fusion
  (49 shorter events, 1.7 us)
Async XLA Ops:
  0.0 41.0 %copy-start = (bf16[2048,512]{1,0:T(8,128)(2,1)S(1)}, bf16[2048,512]{1,0:T(8,128)(2,1)}, u32[]{:S(2)}) copy-start(bf16[2048,512]{1,0:T(8,128)(2,1)} %param.17) | copy-start | bytes 6291460
  2.4 11.4 %copy-start.4 = (bf16[6,8,256]{2,1,0:T(8,128)(2,1)S(1)}, bf16[6,8,256]{2,1,0:T(8,128)(2,1)}, u32[]{:S(2)}) copy-start(bf16[6,8,256]{2,1,0:T(8,128)(2,1)} %param.12) | copy-start | bytes 73732
  2.4 16.8 %copy-start.6 = (bf16[6,4,256]{2,1,0:T(4,128)(2,1)S(1)}, bf16[6,4,256]{2,1,0:T(4,128)(2,1)}, u32[]{:S(2)}) copy-start(bf16[6,4,256]{2,1,0:T(4,128)(2,1)} %param.13) | copy-start | bytes 36868
  2.4 16.9 %copy-start.8 = (s32[6]{0:T(128)S(1)}, s32[6]{0:T(128)}, u32[]{:S(2)}) copy-start(s32[6]{0:T(128)} %param.15) | copy-start | bytes 76
  19.5 5.3 %copy-start.2 = (bf16[6,64,64,128]{3,2,1,0:T(8,128)(2,1)S(1)}, bf16[6,64,64,128]{3,2,1,0:T(8,128)(2,1)}, u32[]{:S(2)}) copy-start(bf16[6,64,64,128]{3,2,1,0:T(8,128)(2,1)} %get-tuple-element.6) | copy-start | bytes 18874372
  25.9 32.3 %copy-start.3 = (bf16[48,512]{1,0:T(8,128)(2,1)S(1)}, bf16[48,512]{1,0:T(8,128)(2,1)}, u32[]{:S(2)}) copy-start(bf16[48,512]{1,0:T(8,128)(2,1)} %param.18) | copy-start | bytes 147460
  25.9 48.0 %copy-start.7 = (f32[512]{0:T(512)S(1)}, f32[512]{0:T(512)}, u32[]{:S(2)}) copy-start(f32[512]{0:T(512)} %param.19) | copy-start | bytes 6148
  41.0 37.6 %copy-start.5 = (f32[48,8]{0,1:T(8,128)S(1)}, f32[48,8]{0,1:T(8,128)}, u32[]{:S(2)}) copy-start(f32[48,8]{0,1:T(8,128)} %param.21) | copy-start | bytes 4612
  75.1 11.7 %all-to-all-start = ((bf16[8,2,12,512]{3,1,2,0:T(2,128)(2,1)}), bf16[8,2,12,512]{3,1,2,0:T(2,128)(2,1)S(1)}, u32[]{:S(2)}, u32[]{:S(2)}) async-start(bf16[8,2,12,512]{3,1,2,0:T(2,128)(2,1)} %copy.77), calls=%async_computation | async-start | bytes 393216 | tf_op jit(solution)/shard_map/all_to_all | solution.py:178
  112.8 38.1 %copy-start.1 = (bf16[2048,512]{1,0:T(8,128)(2,1)S(1)}, bf16[2048,512]{1,0:T(8,128)(2,1)}, u32[]{:S(2)}) copy-start(bf16[2048,512]{1,0:T(8,128)(2,1)} %param.17) | copy-start | bytes 6291460
  123.8 11.7 %all-to-all-start.1 = ((bf16[1,24,8,512]{3,1,0,2:T(8,128)(2,1)}), bf16[1,24,8,512]{3,1,0,2:T(8,128)(2,1)S(1)}, u32[]{:S(2)}, u32[]{:S(2)}) async-start(bf16[1,24,8,512]{3,1,0,2:T(8,128)(2,1)} %copy.82), calls=%async_computation.1 | async-start | bytes 393216 | tf_op jit(solution)/shard_map/all_to_all | solution.py:188
where the time goes:
time: 151 us
  blocking collectives  65.2 us (43%)
  matrix products  42.9 us (28%)
  local copies, waits for them, and re-layouts  16.5 us (11%)
  waiting for transfers between devices  15.8 us (10%)
  starting transfers between devices  6.96 us (5%)
  other arithmetic  3.21 us (2%)
    dot_general x1, matrix products, on_device(): jnp.einsum('ecd,edgf->ecgf', arrived, gate_up_weight, preferred_element_t...  25.9 us
    psum x1, blocking collectives, on_device(): lax.psum(head_terms.astype(jnp.bfloat16), ('sect', 'head'))  16.7 us
    all_gather x1, blocking collectives, on_device(): lax.all_gather(attention, 'batch', axis=0, tiled=True)  15 us
    psum x1, blocking collectives, on_device(): lax.psum(combined.astype(jnp.bfloat16), ('sect', 'head'))  14.6 us
    psum x1, blocking collectives, on_device(): squares = lax.psum(jnp.sum(hidden_state * hidden_state, axis=1), 'batch')  13.6 us
    slice x1, local copies, waits for them, and re-layouts, on_device(): page_cache[..., :head_dim].reshape(seq_count, key_count, head_dim)  11.4 us
    dot_general x1, matrix products, on_device(): jnp.einsum('ecf,efd->ecd', activated, down_weight, preferred_element_type...  10.1 us
    all_to_all x1, waiting for transfers between devices, on_device(): lax.all_to_all(outgoing, 'batch', split_axis=0, concat_axis=3, tiled=True)  8.05 us
  transfers between devices with their start and end apart: 2, of which 2 were waited for; matrix products, arithmetic and copies ran while one was open for 0% of the time, Pallas kernels for 0%

commit v1 on v0

--- a/solution.py
+++ b/solution.py
@@ -1,14 +1,18 @@
+import functools
 import math
 
 import jax
 import jax.numpy as jnp
 from jax import lax
+from jax.experimental import pallas as pl
+from jax.experimental.pallas import tpu as pltpu
 from jax.sharding import PartitionSpec as P
 
 D = 4096
 EXPERTS = 64
 
 
+MESH = pl.DeviceIdType.MESH
 NEG_FILL = -1e30
 NORM_EPS = 1e-06
 
@@ -202,6 +206,368 @@
     return (hidden_state + expert_mix).astype(jnp.bfloat16)
 
 
+NG = 12
+
+
+def layer_kernel(
+    dims,
+    queries_ref, newest_ref, lengths_ref, pages_ref, residual_ref, gain_ref, ids_ref, route_ref,
+    cache_hbm, ow_hbm, gate_hbm, down_hbm,
+    out_ref,
+    cbuf, owbuf, gbuf, dbuf,
+    used_ref, q_out, q_in, attn_all, attn_f32, lhs, psum_buf, hidden_ref, sq_all,
+    sel_ref, sel16, whi_ref, wlo_ref, disp_out, disp_in, x2, acc, act_ref, res_ref,
+    ret_out, ret_in, cb_ref, fin_buf,
+    c_sem, ow_sem, g_sem, d_sem, q_sem, at_s, at_r, p_s, p_r, s_s, s_r, x_s, x_r, r_s, r_r, f_s, f_r,
+):
+    S, B, H, R, CAPN, CH, DC = dims
+    f32, bf16 = jnp.float32, jnp.bfloat16
+    seqs, pages, plen, _ = cbuf.shape
+    hd = cbuf.shape[3] // 2
+    keys = pages * plen
+    tokens, cols = residual_ref.shape
+    group = S * H
+    pairs = gate_hbm.shape[0]
+    depth = gate_hbm.shape[1]
+    ff = gate_hbm.shape[3]
+    nchunk = depth // CH
+    ndown = ff // DC
+    half = cols // 2
+    scaling = 1.0 / math.sqrt(hd)
+    sect, b, h = lax.axis_index("sect"), lax.axis_index("batch"), lax.axis_index("head")
+    pos = sect * H + h
+
+    def cache_copy(i):
+        return pltpu.make_async_copy(cache_hbm.at[i], cbuf.at[i], c_sem.at[i])
+
+    def gate_copy(c):
+        slot = c % NG
+        return pltpu.make_async_copy(
+            gate_hbm.at[c // nchunk, pl.ds((c % nchunk) * CH, CH)], gbuf.at[slot], g_sem.at[slot]
+        )
+
+    def down_copy(c):
+        return pltpu.make_async_copy(
+            down_hbm.at[c // ndown, pl.ds((c % ndown) * DC, DC)], dbuf.at[c], d_sem.at[c]
+        )
+
+    ow_copy = pltpu.make_async_copy(ow_hbm, owbuf, ow_sem)
+    for i in range(seqs):
+        cache_copy(i).start()
+    ow_copy.start()
+
+    barrier = pltpu.get_barrier_semaphore()
+
+    def batch_peer(k):
+        return (sect, lax.rem(b + k, B), h)
+
+    def group_peer(k):
+        p = lax.rem(pos + k, group)
+        return (p // H, b, p % H)
+
+    for k in range(1, B):
+        pl.semaphore_signal(barrier, inc=1, device_id=batch_peer(k), device_id_type=MESH)
+    for k in range(1, group):
+        pl.semaphore_signal(barrier, inc=1, device_id=group_peer(k), device_id_type=MESH)
+
+    q_all = queries_ref[...].astype(f32)
+    q_first, q_second = q_all[:, :, :hd], q_all[:, :, hd:]
+    q_in[h] = jnp.where(h == 0, q_first, q_second)
+    q_out[...] = jnp.where(h == 0, q_second, q_first)
+
+    pl.semaphore_wait(barrier, B - 1 + group - 1)
+
+    q_copy = pltpu.make_async_remote_copy(
+        src_ref=q_out, dst_ref=q_in.at[h], send_sem=q_sem.at[0], recv_sem=q_sem.at[1],
+        device_id=(sect, b, 1 - h), device_id_type=MESH,
+    )
+    q_copy.start()
+
+    chosen = jnp.zeros((seqs, pages_ref.shape[2]), jnp.int32)
+    for k in range(pages_ref.shape[1]):
+        chosen = chosen + jnp.where(pos == k, pages_ref[:, k, :], 0)
+    page_iota = lax.broadcasted_iota(jnp.int32, (seqs, pages), 1)
+    used = jnp.zeros((seqs, pages), f32)
+    for j in range(pages_ref.shape[2]):
+        used = jnp.maximum(used, jnp.where(chosen[:, j : j + 1] == page_iota, 1.0, 0.0))
+    spread_low = lax.broadcasted_iota(jnp.int32, (pages, keys), 0) * plen
+    spread_at = lax.broadcasted_iota(jnp.int32, (pages, keys), 1)
+    spread = jnp.where((spread_at >= spread_low) & (spread_at < spread_low + plen), 1.0, 0.0)
+    used_ref[0:seqs, :] = jnp.dot(used.astype(bf16), spread.astype(bf16), preferred_element_type=f32)
+
+    count = B * pairs
+    slots = count * CAPN
+    expert = 2 * (sect * count + lax.broadcasted_iota(jnp.int32, (count, tokens), 0)) + h
+    route = route_ref[...]
+    coef = route / jnp.sum(route, axis=0, keepdims=True)
+    member = jnp.zeros((count, tokens), f32)
+    amount = jnp.zeros((count, tokens), f32)
+    for k in range(ids_ref.shape[0]):
+        hit = ids_ref[k : k + 1, :] == expert
+        member = jnp.where(hit, 1.0, member)
+        amount = jnp.where(hit, coef[k : k + 1, :], amount)
+    before = jnp.where(
+        lax.broadcasted_iota(jnp.int32, (tokens, tokens), 0)
+        < lax.broadcasted_iota(jnp.int32, (tokens, tokens), 1), 1.0, 0.0
+    )
+    rank = jnp.dot(member.astype(bf16), before.astype(bf16), preferred_element_type=f32)
+    rank = jnp.where(member > 0.5, rank, -1.0)
+    slot_row = lax.broadcasted_iota(jnp.int32, (slots, count), 0)
+    slot_low = lax.broadcasted_iota(jnp.int32, (slots, count), 1) * CAPN
+    widen = jnp.where((slot_row >= slot_low) & (slot_row < slot_low + CAPN), 1.0, 0.0)
+    within = jnp.sum(widen * (slot_row - slot_low).astype(f32), axis=1, keepdims=True)
+    widen = widen.astype(bf16)
+    slot_rank = jnp.dot(widen, rank.astype(bf16), preferred_element_type=f32)
+    sel = jnp.where(slot_rank == within, 1.0, 0.0)
+    sel_ref[...] = sel
+    sel16[...] = sel.astype(bf16)
+    amount_hi = amount.astype(bf16)
+    amount_lo = (amount - amount_hi.astype(f32)).astype(bf16)
+    eye = jnp.where(
+        lax.broadcasted_iota(jnp.int32, (tokens, tokens), 0)
+        == lax.broadcasted_iota(jnp.int32, (tokens, tokens), 1), 1.0, 0.0
+    ).astype(bf16)
+    for part, target in ((amount_hi, whi_ref), (amount_lo, wlo_ref)):
+        rows = (sel * jnp.dot(widen, part, preferred_element_type=f32)).astype(bf16)
+        target[...] = lax.dot_general(
+            eye, rows, (((1,), (1,)), ((), ())), preferred_element_type=f32
+        ).astype(bf16)
+
+    q_copy.wait()
+
+    per_seq = NG // seqs
+
+    @pl.loop(0, seqs)
+    def _(i):
+        cache_copy(i).wait()
+        for n in range(per_seq):
+            gate_copy(i * per_seq + n).start()
+        q = jnp.concatenate([q_in[0, i], q_in[1, i]], axis=0)
+        k_mat = cbuf[i, :, :, 0:hd].reshape(keys, hd)
+        scores = lax.dot_general(
+            q.astype(bf16), k_mat, (((1,), (1,)), ((), ())), preferred_element_type=f32
+        ) * scaling
+        at = lax.broadcasted_iota(jnp.int32, (1, keys), 1)
+        usable = (used_ref[pl.ds(i, 1), :] > 0.5) & (at < lengths_ref[i])
+        fill = jnp.where(usable, 0.0, 1.0)
+        scores = jnp.where(fill > 0.5, NEG_FILL, scores)
+        fresh = newest_ref[i].astype(f32)
+        mine = lax.broadcasted_iota(jnp.int32, fresh.shape, 0) == pos
+        fresh = jnp.sum(jnp.where(mine, fresh, 0.0), axis=0, keepdims=True)
+        fresh_score = jnp.sum(q * fresh[:, :hd], axis=1, keepdims=True) * scaling
+        top = jnp.maximum(jnp.max(scores, axis=1, keepdims=True), fresh_score)
+        weights = jnp.where(fill > 0.5, 0.0, jnp.exp(scores - top))
+        fresh_weight = jnp.exp(fresh_score - top)
+        total = jnp.sum(weights, axis=1, keepdims=True) + fresh_weight
+        v_mat = cbuf[i, :, :, hd : 2 * hd].reshape(keys, hd)
+        mixed = jnp.dot(weights.astype(bf16), v_mat, preferred_element_type=f32)
+        mixed = mixed + fresh_weight.astype(bf16).astype(f32) * fresh[:, hd:]
+        attn_all[b, i] = (mixed / total).astype(bf16)
+
+    def to_batch(src_at, dst, send_sem, recv_sem):
+        copies = []
+        for k in range(1, B):
+            peer = batch_peer(k)
+            copies.append(
+                pltpu.make_async_remote_copy(
+                    src_ref=src_at(peer[1]), dst_ref=dst.at[b],
+                    send_sem=send_sem.at[k - 1], recv_sem=recv_sem.at[k - 1],
+                    device_id=peer, device_id_type=MESH,
+                )
+            )
+        for copy in copies:
+            copy.start()
+        return copies
+
+    def to_group(buf, send_sem, recv_sem):
+        copies = []
+        for k in range(1, group):
+            copies.append(
+                pltpu.make_async_remote_copy(
+                    src_ref=buf.at[pos], dst_ref=buf.at[pos],
+                    send_sem=send_sem.at[k - 1], recv_sem=recv_sem.at[k - 1],
+                    device_id=group_peer(k), device_id_type=MESH,
+                )
+            )
+        for copy in copies:
+            copy.start()
+        return copies
+
+    def finish(copies):
+        for copy in copies:
+            copy.wait()
+
+    gather = to_batch(lambda peer: attn_all.at[b], attn_all, at_s, at_r)
+
+    @pl.loop(0, pairs * ndown)
+    def _(c):
+        down_copy(c).start()
+
+    finish(gather)
+
+    heads = attn_all.shape[2]
+    attn_f32[...] = attn_all[...].reshape(tokens, heads, hd).astype(f32)
+    for j in range(heads):
+        lhs[:, j * hd : (j + 1) * hd] = attn_f32[:, j, :].astype(bf16)
+    ow_copy.wait()
+    psum_buf[pos] = jnp.dot(lhs[...], owbuf[...], preferred_element_type=f32).astype(bf16)
+    finish(to_group(psum_buf, p_s, p_r))
+    projected = psum_buf[0].astype(f32)
+    for p in range(1, group):
+        projected = projected + psum_buf[p].astype(f32)
+    hidden = residual_ref[...].astype(f32) + projected
+    hidden_ref[...] = hidden
+
+    gained = (hidden * gain_ref[...].reshape(1, cols)).astype(bf16)
+    picked = jnp.dot(sel16[...], gained, preferred_element_type=f32)
+    for t in range(B):
+        piece = picked[t * R : (t + 1) * R]
+        disp_out[t] = jnp.concatenate([piece[:, :half], piece[:, half:]], axis=0).astype(bf16)
+    dispatch = to_batch(lambda peer: disp_out.at[peer], disp_in, x_s, x_r)
+    squares = jnp.sum(hidden * hidden, axis=1, keepdims=True)
+    diag = lax.broadcasted_iota(jnp.int32, (tokens, 128), 0) == lax.broadcasted_iota(
+        jnp.int32, (tokens, 128), 1
+    )
+    sq_row = jnp.sum(jnp.where(diag, squares, 0.0), axis=0, keepdims=True)
+    sq_all[b] = jnp.broadcast_to(sq_row, (8, 128))
+    sq_copies = to_batch(lambda peer: sq_all.at[b], sq_all, s_s, s_r)
+    disp_in[b] = disp_out[b]
+    z_row = 2 * lax.broadcasted_iota(jnp.int32, (128, 512), 0)
+    z_col = lax.broadcasted_iota(jnp.int32, (128, 512), 1)
+    place = jnp.where((z_col == z_row) | (z_col == z_row + 257), 1.0, 0.0).astype(bf16)
+    finish(dispatch)
+
+    @pl.loop(0, B)
+    def _(s):
+        got = disp_in[s].astype(f32)
+        pieces = []
+        for n in range(cols // 128):
+            top_row = 0 if n * 128 < half else R
+            at = n * 128 % half
+            pieces.append(got[top_row : top_row + R, at : at + 128])
+        spread_x = jnp.dot(
+            jnp.concatenate(pieces, axis=0).astype(bf16), place, preferred_element_type=f32
+        )
+        for n in range(cols // 128):
+            rows = spread_x[n * R : (n + 1) * R]
+            to = pl.multiple_of(s * (2 * cols) + n * 256, 256)
+            x2[:, pl.ds(to, 256)] = jnp.concatenate(
+                [rows[:, :256], rows[:, 256:]], axis=0
+            ).astype(bf16)
+
+    finish(sq_copies)
+    sq_total = sq_all[0]
+    for t in range(1, B):
+        sq_total = sq_total + sq_all[t]
+    inverse = lax.rsqrt(sq_total / D + NORM_EPS)[0:1, 0:tokens]
+    own = sel_ref[pl.ds(pl.multiple_of(b * R, 8), R), :]
+    row_inverse = jnp.sum(own * inverse, axis=1, keepdims=True)
+    row_number = lax.broadcasted_iota(jnp.int32, (R, ff), 0)
+
+    res_ref[...] = jnp.zeros_like(res_ref)
+    for e in range(pairs):
+        acc[...] = jnp.zeros_like(acc)
+
+        @pl.loop(0, nchunk)
+        def _(c):
+            at = e * nchunk + c
+            gate_copy(at).wait()
+            weight = gbuf.at[at % NG].reshape(2 * CH, ff)
+            left = x2[:, pl.ds(pl.multiple_of(c * (2 * CH), 2 * CH), 2 * CH)]
+            acc[...] += jnp.dot(left, weight[...], preferred_element_type=f32)
+
+            @pl.when(at + NG < pairs * nchunk)
+            def _():
+                gate_copy(at + NG).start()
+
+        gate = acc[0:R] * row_inverse
+        up = acc[R : 2 * R] * row_inverse
+        value = gate * (1.0 / (1.0 + jnp.exp(-gate))) * up
+        held = (row_number >= e * CAPN) & (row_number < (e + 1) * CAPN)
+        act_ref[...] = jnp.where(held, value, 0.0).astype(bf16)
+
+        @pl.loop(0, ndown)
+        def _(c):
+            at = e * ndown + c
+            down_copy(at).wait()
+            left = act_ref[:, pl.ds(pl.multiple_of(c * DC, DC), DC)]
+            res_ref[...] += jnp.dot(left, dbuf[at], preferred_element_type=f32)
+
+    for t in range(B):
+        piece = res_ref[:, t * cols : (t + 1) * cols]
+        ret_out[t] = jnp.concatenate([piece[:, :half], piece[:, half:]], axis=0).astype(bf16)
+    back = to_batch(lambda peer: ret_out.at[peer], ret_in, r_s, r_r)
+    ret_in[b] = ret_out[b]
+    finish(back)
+    for t in range(B):
+        piece = ret_in[t].astype(f32)
+        cb_ref[t * R : (t + 1) * R, :half] = piece[:R]
+        cb_ref[t * R : (t + 1) * R, half:] = piece[R:]
+    came = cb_ref[...].astype(bf16)
+    combined = jnp.dot(whi_ref[...], came, preferred_element_type=f32) + jnp.dot(
+        wlo_ref[...], came, preferred_element_type=f32
+    )
+    fin_buf[pos] = combined.astype(bf16)
+    finish(to_group(fin_buf, f_s, f_r))
+    mix = fin_buf[0].astype(f32)
+    for p in range(1, group):
+        mix = mix + fin_buf[p].astype(f32)
+    out_ref[...] = (hidden_ref[...] + mix).astype(out_ref.dtype)
+
+
+def fused(
+    queries, newest, cache, lengths, page_ids, out_weight, residual, gain, ids, route, gate_up, down
+):
+    S, B, H = lax.axis_size("sect"), lax.axis_size("batch"), lax.axis_size("head")
+    seqs, qh, _ = queries.shape
+    hd = newest.shape[2] // 2
+    tokens, cols = residual.shape
+    pairs, depth, _, ff = gate_up.shape
+    capn = 2 * tokens * ids.shape[1] // EXPERTS
+    R = pairs * capn
+    CH, DC = 256, 256
+    keys = cache.shape[1] * cache.shape[2]
+    slots = B * R
+    group = S * H
+    bf16, f32 = jnp.bfloat16, jnp.float32
+    V, dma = pltpu.VMEM, pltpu.SemaphoreType.DMA
+    vm, hbm = pl.BlockSpec(memory_space=pltpu.VMEM), pl.BlockSpec(memory_space=pl.ANY)
+    smem = pl.BlockSpec(memory_space=pltpu.SMEM)
+    ndown = ff // DC
+    return pl.pallas_call(
+        functools.partial(layer_kernel, (S, B, H, R, capn, CH, DC)),
+        out_shape=jax.ShapeDtypeStruct((tokens, cols), bf16),
+        in_specs=[vm, vm, smem, vm, vm, vm, vm, vm, hbm, hbm, hbm, hbm],
+        out_specs=vm,
+        scratch_shapes=[
+            V(cache.shape, bf16), V(out_weight.shape, bf16), V((NG, CH, 2, ff), bf16),
+            V((pairs * ndown, DC, depth), bf16),
+            V((-(-seqs // 8) * 8, keys), f32), V((seqs, qh, hd), f32), V((H, seqs, qh, hd), f32),
+            V((B, seqs, qh * H, hd), bf16), V((tokens, qh * H, hd), f32),
+            V((tokens, qh * H * hd), bf16), V((group, tokens, cols), bf16), V((tokens, cols), f32),
+            V((B, 8, 128), f32),
+            V((slots, tokens), f32), V((slots, tokens), bf16), V((tokens, slots), bf16),
+            V((tokens, slots), bf16), V((B, 2 * R, cols // 2), bf16),
+            V((B, 2 * R, cols // 2), bf16), V((2 * R, 2 * depth), bf16), V((2 * R, ff), f32),
+            V((R, ff), bf16), V((R, depth), f32),
+            V((B, 2 * R, cols // 2), bf16), V((B, 2 * R, cols // 2), bf16), V((slots, cols), f32),
+            V((group, tokens, cols), bf16),
+            dma((seqs,)), dma, dma((NG,)), dma((pairs * ndown,)), dma((2,)),
+            dma((B - 1,)), dma((B - 1,)), dma((group - 1,)), dma((group - 1,)),
+            dma((B - 1,)), dma((B - 1,)), dma((B - 1,)), dma((B - 1,)),
+            dma((B - 1,)), dma((B - 1,)), dma((group - 1,)), dma((group - 1,)),
+        ],
+        compiler_params=pltpu.CompilerParams(
+            collective_id=0, has_side_effects=True, vmem_limit_bytes=63 * 1024 * 1024
+        ),
+        cost_estimate=pl.CostEstimate(
+            flops=4 * R * depth * ff * pairs * 3,
+            bytes_accessed=2 * (gate_up.size + down.size + cache.size), transcendentals=0,
+        ),
+    )(queries, newest, lengths, page_ids, residual, gain, ids.T, route.T,
+      cache, out_weight, gate_up, down)
+
+
 def solution(mesh):
     placed = (
         P("batch", "head", "sect"),
@@ -217,6 +583,8 @@
         P(("sect", "batch"), None, None, "head"),
         P(("sect", "batch"), "head", None),
     )
+    whole_parts = mesh.shape["sect"] * mesh.shape["head"] == 4 and mesh.shape["head"] == 2
+    body = fused if whole_parts else on_device
     return jax.shard_map(
-        on_device, mesh=mesh, in_specs=placed, out_specs=P(None, "batch"), check_vma=False
-    )
+        body, mesh=mesh, in_specs=placed, out_specs=P(None, "batch"), check_vma=False
+    )

time: 151 us -> 64 us (0.42)
  blocking collectives: 65.2 us -> 0 us
  Pallas kernels: 0 us -> 62.3 us
  matrix products: 42.9 us -> 0 us
  waiting for transfers between devices: 15.8 us -> 0 us
  local copies, waits for them, and re-layouts: 16.5 us -> 1.42 us
  starting transfers between devices: 6.96 us -> 0 us
  other arithmetic: 3.21 us -> 0 us
    pallas_call x0 -> x1, Pallas kernels: none -> 62.3 us  [fused(): pl.pallas_call(functools.partial(layer_kernel, (S, B, H, R, capn, CH, DC)...]
    psum x3 -> x0, blocking collectives: 44.8 us -> none  [the longest x1 16.7 us: on_device(): lax.psum(head_terms.astype(jnp.bfloat16), ('sect', 'head'))]
    dot_general x8 -> x0, matrix products: 42.9 us -> none  [the longest x1 25.9 us: on_device(): jnp.einsum('ecd,edgf->ecgf', arrived, gate_up_weight, preferred_element_t...]
    all_gather x2 -> x0, blocking collectives: 20.4 us -> none  [the longest x1 15 us: on_device(): lax.all_gather(attention, 'batch', axis=0, tiled=True)]
    all_to_all x2 -> x0, waiting for transfers between devices: 15.8 us -> none  [the longest x1 8.05 us: on_device(): lax.all_to_all(outgoing, 'batch', split_axis=0, concat_axis=3, tiled=True)]
    slice x2 -> x0, local copies, waits for them, and re-layouts: 11.6 us -> none  [the longest x1 11.4 us: on_device(): page_cache[..., :head_dim].reshape(seq_count, key_count, head_dim)]
    all_to_all x2 -> x0, starting transfers between devices: 6.96 us -> none  [the longest x1 3.57 us: on_device(): lax.all_to_all(outgoing, 'batch', split_axis=0, concat_axis=3, tiled=True)]
  transfers between devices with their start and end apart: 2 -> 0, of which waited for: 2 -> 0; matrix products, arithmetic and copies ran while one was open for 0% -> 0% of each run, Pallas kernels for 0% -> 0%
where the time goes in v1:
time: 64 us; the launch traced here: 63.8 us
  Pallas kernels  62.3 us (97%)
  local copies, waits for them, and re-layouts  1.42 us (2%)
    pallas_call x1, Pallas kernels, fused(): pl.pallas_call(functools.partial(layer_kernel, (S, B, H, R, capn, CH, DC)...  62.3 us
    unnamed x1, local copies, waits for them, and re-layouts  1.42 us

profile of v1, /device:TPU:0, one launch (start us, length us, event | category | flops | bytes accessed | tf_op | source)
XLA Modules:
  0.0 63.8 jit_solution(15552173237677114397)
XLA Ops:
  0.0 62.3 %shard_map.118 = bf16[48,512]{1,0:T(8,128)(2,1)} custom-call(bf16[6,8,256]{2,1,0:T(8,128)(2,1)} %queries_ref.1, bf16[6,4,256]{2,1,0:T(4,128)(2,1)} %newest_ref.1, s32[6]{0:T(128)} %lengths_ref.1, s32[6,4,32]{2,1,0:T(4,128)} %pages_ref.1, bf16[48,512]{1,0:T(8,128)(2,1)} %residual_ref.1, f32[512]{0:T(512)} %gain_ref.1, s32[8,48]{1,0:T(8,128)} %bitcast.2, ...), custom_call_target="tpu_custom_call" | custom-call | flops 3623878656 | bytes 88080384 | tf_op jit(solution)/shard_map/pallas_call | solution.py:537
  62.3 1.4 %copy.14 = bf16[48,512]{1,0:T(8,128)(2,1)} copy(bf16[48,512]{1,0:T(8,128)(2,1)} %shard_map.118) | data formatting | bytes 98304

commit v2 on v1

--- a/solution.py
+++ b/solution.py
@@ -206,7 +206,9 @@
     return (hidden_state + expert_mix).astype(jnp.bfloat16)
 
 
-NG = 12
+NG = 7
+CACHE_SLOTS = 3
+BACK_ROWS = 16
 
 
 def layer_kernel(
@@ -222,8 +224,9 @@
 ):
     S, B, H, R, CAPN, CH, DC = dims
     f32, bf16 = jnp.float32, jnp.bfloat16
-    seqs, pages, plen, _ = cbuf.shape
+    seqs, pages, plen, _ = cache_hbm.shape
     hd = cbuf.shape[3] // 2
+    slots_c = cbuf.shape[0]
     keys = pages * plen
     tokens, cols = residual_ref.shape
     group = S * H
@@ -238,12 +241,13 @@
     pos = sect * H + h
 
     def cache_copy(i):
-        return pltpu.make_async_copy(cache_hbm.at[i], cbuf.at[i], c_sem.at[i])
+        return pltpu.make_async_copy(cache_hbm.at[i], cbuf.at[i % slots_c], c_sem.at[i % slots_c])
 
     def gate_copy(c):
         slot = c % NG
         return pltpu.make_async_copy(
-            gate_hbm.at[c // nchunk, pl.ds((c % nchunk) * CH, CH)], gbuf.at[slot], g_sem.at[slot]
+            gate_hbm.at[c // nchunk, pl.ds((c % nchunk) * CH, CH)], gbuf.at[slot, :, :, pl.ds(0, ff)],
+            g_sem.at[slot],
         )
 
     def down_copy(c):
@@ -252,7 +256,7 @@
         )
 
     ow_copy = pltpu.make_async_copy(ow_hbm, owbuf, ow_sem)
-    for i in range(seqs):
+    for i in range(slots_c):
         cache_copy(i).start()
     ow_copy.start()
 
@@ -335,15 +339,11 @@
 
     q_copy.wait()
 
-    per_seq = NG // seqs
-
-    @pl.loop(0, seqs)
-    def _(i):
+    def attend(i):
         cache_copy(i).wait()
-        for n in range(per_seq):
-            gate_copy(i * per_seq + n).start()
+        held = cbuf.at[i % slots_c]
         q = jnp.concatenate([q_in[0, i], q_in[1, i]], axis=0)
-        k_mat = cbuf[i, :, :, 0:hd].reshape(keys, hd)
+        k_mat = held[:, :, 0:hd].reshape(keys, hd)
         scores = lax.dot_general(
             q.astype(bf16), k_mat, (((1,), (1,)), ((), ())), preferred_element_type=f32
         ) * scaling
@@ -359,19 +359,23 @@
         weights = jnp.where(fill > 0.5, 0.0, jnp.exp(scores - top))
         fresh_weight = jnp.exp(fresh_score - top)
         total = jnp.sum(weights, axis=1, keepdims=True) + fresh_weight
-        v_mat = cbuf[i, :, :, hd : 2 * hd].reshape(keys, hd)
+        v_mat = held[:, :, hd : 2 * hd].reshape(keys, hd)
         mixed = jnp.dot(weights.astype(bf16), v_mat, preferred_element_type=f32)
         mixed = mixed + fresh_weight.astype(bf16).astype(f32) * fresh[:, hd:]
         attn_all[b, i] = (mixed / total).astype(bf16)
 
-    def to_batch(src_at, dst, send_sem, recv_sem):
+        @pl.when(i + slots_c < seqs)
+        def _():
+            cache_copy(i + slots_c).start()
+
+    def to_batch(src_at, dst_at, send_sem, recv_sem, first=0):
         copies = []
         for k in range(1, B):
             peer = batch_peer(k)
             copies.append(
                 pltpu.make_async_remote_copy(
-                    src_ref=src_at(peer[1]), dst_ref=dst.at[b],
-                    send_sem=send_sem.at[k - 1], recv_sem=recv_sem.at[k - 1],
+                    src_ref=src_at(peer[1]), dst_ref=dst_at,
+                    send_sem=send_sem.at[first + k - 1], recv_sem=recv_sem.at[first + k - 1],
                     device_id=peer, device_id_type=MESH,
                 )
             )
@@ -397,7 +401,23 @@
         for copy in copies:
             copy.wait()
 
-    gather = to_batch(lambda peer: attn_all.at[b], attn_all, at_s, at_r)
+    part = seqs // 2
+
+    @pl.loop(0, part)
+    def _(i):
+        attend(i)
+
+    early = attn_all.at[b, pl.ds(0, part)]
+    gather = to_batch(lambda peer: early, early, at_s, at_r)
+    for c in range(NG):
+        gate_copy(c).start()
+
+    @pl.loop(part, seqs)
+    def _(i):
+        attend(i)
+
+    late = attn_all.at[b, pl.ds(part, seqs - part)]
+    gather = gather + to_batch(lambda peer: late, late, at_s, at_r, B - 1)
 
     @pl.loop(0, pairs * ndown)
     def _(c):
@@ -423,14 +443,14 @@
     for t in range(B):
         piece = picked[t * R : (t + 1) * R]
         disp_out[t] = jnp.concatenate([piece[:, :half], piece[:, half:]], axis=0).astype(bf16)
-    dispatch = to_batch(lambda peer: disp_out.at[peer], disp_in, x_s, x_r)
+    dispatch = to_batch(lambda peer: disp_out.at[peer], disp_in.at[b], x_s, x_r)
     squares = jnp.sum(hidden * hidden, axis=1, keepdims=True)
     diag = lax.broadcasted_iota(jnp.int32, (tokens, 128), 0) == lax.broadcasted_iota(
         jnp.int32, (tokens, 128), 1
     )
     sq_row = jnp.sum(jnp.where(diag, squares, 0.0), axis=0, keepdims=True)
     sq_all[b] = jnp.broadcast_to(sq_row, (8, 128))
-    sq_copies = to_batch(lambda peer: sq_all.at[b], sq_all, s_s, s_r)
+    sq_copies = to_batch(lambda peer: sq_all.at[b], sq_all.at[b], s_s, s_r)
     disp_in[b] = disp_out[b]
     z_row = 2 * lax.broadcasted_iota(jnp.int32, (128, 512), 0)
     z_col = lax.broadcasted_iota(jnp.int32, (128, 512), 1)
@@ -464,17 +484,18 @@
     row_inverse = jnp.sum(own * inverse, axis=1, keepdims=True)
     row_number = lax.broadcasted_iota(jnp.int32, (R, ff), 0)
 
-    res_ref[...] = jnp.zeros_like(res_ref)
+    back = []
     for e in range(pairs):
+        res_ref[...] = jnp.zeros_like(res_ref)
         acc[...] = jnp.zeros_like(acc)
 
         @pl.loop(0, nchunk)
         def _(c):
             at = e * nchunk + c
             gate_copy(at).wait()
-            weight = gbuf.at[at % NG].reshape(2 * CH, ff)
+            weight = gbuf.at[at % NG].reshape(2 * CH, ff + 128)
             left = x2[:, pl.ds(pl.multiple_of(c * (2 * CH), 2 * CH), 2 * CH)]
-            acc[...] += jnp.dot(left, weight[...], preferred_element_type=f32)
+            acc[...] += jnp.dot(left, weight[:, 0:ff], preferred_element_type=f32)
 
             @pl.when(at + NG < pairs * nchunk)
             def _():
@@ -493,16 +514,20 @@
             left = act_ref[:, pl.ds(pl.multiple_of(c * DC, DC), DC)]
             res_ref[...] += jnp.dot(left, dbuf[at], preferred_element_type=f32)
 
-    for t in range(B):
-        piece = res_ref[:, t * cols : (t + 1) * cols]
-        ret_out[t] = jnp.concatenate([piece[:, :half], piece[:, half:]], axis=0).astype(bf16)
-    back = to_batch(lambda peer: ret_out.at[peer], ret_in, r_s, r_r)
-    ret_in[b] = ret_out[b]
+        low = e * CAPN // 8 * 8
+        for t in range(B):
+            ret_out[e, t] = res_ref[low : low + BACK_ROWS, t * cols : (t + 1) * cols].astype(bf16)
+        back = back + to_batch(
+            lambda peer: ret_out.at[e, peer], ret_in.at[e, b], r_s, r_r, e * (B - 1)
+        )
+        ret_in[e, b] = ret_out[e, b]
+
+    cb_ref[...] = jnp.zeros_like(cb_ref)
     finish(back)
-    for t in range(B):
-        piece = ret_in[t].astype(f32)
-        cb_ref[t * R : (t + 1) * R, :half] = piece[:R]
-        cb_ref[t * R : (t + 1) * R, half:] = piece[R:]
+    for e in range(pairs):
+        low = e * CAPN // 8 * 8
+        for t in range(B):
+            cb_ref[t * R + low : t * R + low + BACK_ROWS] += ret_in[e, t].astype(f32)
     came = cb_ref[...].astype(bf16)
     combined = jnp.dot(whi_ref[...], came, preferred_element_type=f32) + jnp.dot(
         wlo_ref[...], came, preferred_element_type=f32
@@ -525,7 +550,7 @@
     pairs, depth, _, ff = gate_up.shape
     capn = 2 * tokens * ids.shape[1] // EXPERTS
     R = pairs * capn
-    CH, DC = 256, 256
+    CH, DC = 512, 256
     keys = cache.shape[1] * cache.shape[2]
     slots = B * R
     group = S * H
@@ -540,7 +565,8 @@
         in_specs=[vm, vm, smem, vm, vm, vm, vm, vm, hbm, hbm, hbm, hbm],
         out_specs=vm,
         scratch_shapes=[
-            V(cache.shape, bf16), V(out_weight.shape, bf16), V((NG, CH, 2, ff), bf16),
+            V((CACHE_SLOTS,) + cache.shape[1:], bf16), V(out_weight.shape, bf16),
+            V((NG, CH, 2, ff + 128), bf16),
             V((pairs * ndown, DC, depth), bf16),
             V((-(-seqs // 8) * 8, keys), f32), V((seqs, qh, hd), f32), V((H, seqs, qh, hd), f32),
             V((B, seqs, qh * H, hd), bf16), V((tokens, qh * H, hd), f32),
@@ -550,12 +576,13 @@
             V((tokens, slots), bf16), V((B, 2 * R, cols // 2), bf16),
             V((B, 2 * R, cols // 2), bf16), V((2 * R, 2 * depth), bf16), V((2 * R, ff), f32),
             V((R, ff), bf16), V((R, depth), f32),
-            V((B, 2 * R, cols // 2), bf16), V((B, 2 * R, cols // 2), bf16), V((slots, cols), f32),
+            V((pairs, B, BACK_ROWS, cols), bf16), V((pairs, B, BACK_ROWS, cols), bf16),
+            V((slots, cols), f32),
             V((group, tokens, cols), bf16),
-            dma((seqs,)), dma, dma((NG,)), dma((pairs * ndown,)), dma((2,)),
-            dma((B - 1,)), dma((B - 1,)), dma((group - 1,)), dma((group - 1,)),
+            dma((CACHE_SLOTS,)), dma, dma((NG,)), dma((pairs * ndown,)), dma((2,)),
+            dma((2 * (B - 1),)), dma((2 * (B - 1),)), dma((group - 1,)), dma((group - 1,)),
             dma((B - 1,)), dma((B - 1,)), dma((B - 1,)), dma((B - 1,)),
-            dma((B - 1,)), dma((B - 1,)), dma((group - 1,)), dma((group - 1,)),
+            dma((pairs * (B - 1),)), dma((pairs * (B - 1),)), dma((group - 1,)), dma((group - 1,)),
         ],
         compiler_params=pltpu.CompilerParams(
             collective_id=0, has_side_effects=True, vmem_limit_bytes=63 * 1024 * 1024

time: 64 us -> 60.2 us (0.941)
  Pallas kernels: 62.3 us -> 58.5 us
    pallas_call x1, Pallas kernels: 62.3 us -> 58.5 us  [fused(): pl.pallas_call(functools.partial(layer_kernel, (S, B, H, R, capn, CH, DC)...]
where the time goes in v2:
time: 60.2 us; the launch traced here: 59.9 us
  Pallas kernels  58.5 us (97%)
  local copies, waits for them, and re-layouts  1.42 us (2%)
    pallas_call x1, Pallas kernels, fused(): pl.pallas_call(functools.partial(layer_kernel, (S, B, H, R, capn, CH, DC)...  58.5 us
    unnamed x1, local copies, waits for them, and re-layouts  1.42 us

profile of v2, /device:TPU:0, one launch (start us, length us, event | category | flops | bytes accessed | tf_op | source)
XLA Modules:
  0.0 59.9 jit_solution(1314926680647226557)
XLA Ops:
  0.0 58.5 %shard_map.118 = bf16[48,512]{1,0:T(8,128)(2,1)} custom-call(bf16[6,8,256]{2,1,0:T(8,128)(2,1)} %queries_ref.1, bf16[6,4,256]{2,1,0:T(4,128)(2,1)} %newest_ref.1, s32[6]{0:T(128)} %lengths_ref.1, s32[6,4,32]{2,1,0:T(4,128)} %pages_ref.1, bf16[48,512]{1,0:T(8,128)(2,1)} %residual_ref.1, f32[512]{0:T(512)} %gain_ref.1, s32[8,48]{1,0:T(8,128)} %bitcast.2, ...), custom_call_target="tpu_custom_call" | custom-call | flops 3623878656 | bytes 88080384 | tf_op jit(solution)/shard_map/pallas_call | solution.py:562
  58.5 1.4 %copy.14 = bf16[48,512]{1,0:T(8,128)(2,1)} copy(bf16[48,512]{1,0:T(8,128)(2,1)} %shard_map.118) | data formatting | bytes 98304
